TPU v7x, 32 devices: a whole 2x2x4 slice. The times are simulated.
32 devices in a mesh: dp: 4 (over x, core), ctx: 8 (over z, y).
Axes of the slice: x: 2, y: 2, z: 4, core: 2. Of those that a mesh axis runs over, the one named last changes fastest.
Arguments:
- tokens_in: bfloat16 [4, 2048, 960], P('dp', 'ctx'), may hold values from -6 to 6
- cotangent: bfloat16 [4, 2048, 960], P('dp', 'ctx'), may hold values from -6 to 6
- w_query: bfloat16 [921600], P(('dp', 'ctx')), may hold values from -0.25 to 0.25
- w_key: bfloat16 [307200], P(('dp', 'ctx')), may hold values from -0.25 to 0.25
- w_value: bfloat16 [307200], P(('dp', 'ctx')), may hold values from -0.1875 to 0.1875
- w_output: bfloat16 [921600], P(('dp', 'ctx')), may hold values from -0.75 to 0.75
- w_gate: bfloat16 [2457600], P(('dp', 'ctx')), may hold values from -0.1875 to 0.1875
- w_up: bfloat16 [2457600], P(('dp', 'ctx')), may hold values from -0.1875 to 0.1875
- w_down: bfloat16 [2457600], P(('dp', 'ctx')), may hold values from -0.15625 to 0.15625
- norm_gains: bfloat16 [2, 960], replicated, may hold values from 0.25 to 1.75
- seq_lengths: int32 [4, 3], P('dp'), may hold values from 32 to 1920, as said below
- block_order: int32 [4, 16], P('dp'), may hold values from 0 to 15, as said below
Outputs:
- block_out: float32 [4, 2048, 960], P('dp', 'ctx')
- grad_input: float32 [4, 2048, 960], P('dp', 'ctx')
- grad_query: float32 [921600], P(('dp', 'ctx'))
- grad_key: float32 [307200], P(('dp', 'ctx'))
- grad_value: float32 [307200], P(('dp', 'ctx'))
- grad_output: float32 [921600], P(('dp', 'ctx'))
- grad_gate: float32 [2457600], P(('dp', 'ctx'))
- grad_up: float32 [2457600], P(('dp', 'ctx'))
- grad_down: float32 [2457600], P(('dp', 'ctx'))
- grad_gains: float32 [2, 960], replicated
Inputs may be any that keep to these rules, and one draw needn't show every extreme that they name: `seq_lengths`: each group has one document, at a place drawn from the seed, of 1920 tokens; the other two together have 128 tokens. `block_order`: each row is a permutation of the group's blocks; the first stored block of the first device of ctx, the first stored block of the device at index 4 of ctx, and the last stored block of the last device of ctx hold the packed blocks second, third and fourth from the end.
All inputs are finite; a program needn't handle non-finite values.
Results may differ from a plain program's by a relative error of at most 0.018.
Values may be sent and summed in bfloat16 or wider, within the bound.
A program may use at most 256 MiB of HBM per device.

v0:
```python
import jax
import jax.numpy as jnp
from jax import lax
from jax.sharding import PartitionSpec as P

D = 960
HEADS = 15
KV_HEADS = 5
HEAD_DIM = 64
FF = 2560
BLOCK = 128
SEQS = 3
Q_WIDTH = 960
KV_WIDTH = 320


def rms_scale(values):
    return lax.rsqrt(jnp.mean(values * values, axis=-1, keepdims=True) + 1e-05)


def frequencies():
    half_dim = HEAD_DIM // 2
    return 10000.0 ** (-(2.0 * jnp.arange(half_dim).astype(jnp.float32)) / HEAD_DIM)


def rotary(values, angles):
    half_dim = values.shape[-1] // 2
    first = values[..., :half_dim]
    second = values[..., half_dim:]
    cosine = jnp.cos(angles)[:, None, :]
    sine = jnp.sin(angles)[:, None, :]
    return jnp.concatenate(
        [first * cosine - second * sine, second * cosine + first * sine], axis=-1
    )


def token_tables(lengths, arrangement):
    ends = jnp.cumsum(lengths)
    starts = ends - lengths
    logical = (arrangement[:, None] * BLOCK + jnp.arange(BLOCK, dtype=jnp.int32)[None, :]).reshape(
        -1
    )
    document = jnp.sum((logical[:, None] >= ends[None, :]).astype(jnp.int32), axis=1)
    chosen = document[:, None] == jnp.arange(SEQS, dtype=jnp.int32)[None, :]
    offset = jnp.sum(jnp.where(chosen, starts[None, :], 0), axis=1)
    return (logical, document, logical - offset)


def matmul(left, right):
    return jnp.dot(left, right, preferred_element_type=jnp.float32)


def outer_sum(left, right):
    return lax.dot_general(
        left, right, (((0,), (0,)), ((), ())), preferred_element_type=jnp.float32
    )


def back_dot(grad_rows, weight):
    return lax.dot_general(
        grad_rows, weight, (((1,), (1,)), ((), ())), preferred_element_type=jnp.float32
    )


def norm_back(grad_normed, base_normed, inv_scale, gain_row):
    scaled = grad_normed * gain_row
    grad_rows = inv_scale * (
        scaled - base_normed * jnp.mean(scaled * base_normed, axis=-1, keepdims=True)
    )
    return (grad_rows, jnp.sum(grad_normed * base_normed, axis=0))


def local(
    tokens_in,
    cotangent,
    w_query,
    w_key,
    w_value,
    w_output,
    w_gate,
    w_up,
    w_down,
    norm_gains,
    seq_lengths,
    block_order,
):
    row_count = tokens_in.shape[1]
    repeat = HEADS // KV_HEADS
    score_scale = HEAD_DIM ** (-0.5)
    shapes = ((D, Q_WIDTH), (D, KV_WIDTH), (D, KV_WIDTH), (Q_WIDTH, D), (D, FF), (D, FF), (FF, D))
    gathered = (
        lax.all_gather(w_query, ("dp", "ctx"), axis=0, tiled=True),
        lax.all_gather(w_key, ("dp", "ctx"), axis=0, tiled=True),
        lax.all_gather(w_value, ("dp", "ctx"), axis=0, tiled=True),
        lax.all_gather(w_output, ("dp", "ctx"), axis=0, tiled=True),
        lax.all_gather(w_gate, ("dp", "ctx"), axis=0, tiled=True),
        lax.all_gather(w_up, ("dp", "ctx"), axis=0, tiled=True),
        lax.all_gather(w_down, ("dp", "ctx"), axis=0, tiled=True),
    )
    full_query, full_key, full_value, full_output, full_gate, full_up, full_down = tuple(
        (flat.reshape(shape_pair) for flat, shape_pair in zip(gathered, shapes))
    )
    lengths = seq_lengths[0]
    arrangement = block_order[0]
    logical_all, document_all, position_all = token_tables(lengths, arrangement)
    group_total = logical_all.shape[0]
    block_total = arrangement.shape[0]
    first_row = lax.axis_index("ctx") * row_count
    own_logical = lax.dynamic_slice_in_dim(logical_all, first_row, row_count)
    own_document = lax.dynamic_slice_in_dim(document_all, first_row, row_count)
    own_position = lax.dynamic_slice_in_dim(position_all, first_row, row_count)
    angles = own_position.astype(jnp.float32)[:, None] * frequencies()[None, :]
    low_block = jnp.min(own_logical - own_position) // BLOCK
    high_block = jnp.max(own_logical) // BLOCK + 1
    ends = jnp.cumsum(lengths)
    packed_index = jnp.arange(group_total, dtype=jnp.int32)
    packed_document = jnp.sum((packed_index[:, None] >= ends[None, :]).astype(jnp.int32), axis=1)
    block_ids = jnp.arange(block_total, dtype=jnp.int32)
    stored_of_packed = jnp.sum(
        jnp.where(arrangement[None, :] == block_ids[:, None], block_ids[None, :], 0), axis=1
    )
    tokens = tokens_in[0].astype(jnp.float32)
    gains = norm_gains.astype(jnp.float32)
    inv_one = rms_scale(tokens)
    base_one = tokens * inv_one
    normed = (base_one * gains[0]).astype(jnp.bfloat16)
    query_proj = matmul(normed, full_query).reshape(row_count, HEADS, HEAD_DIM)
    queries = (
        rotary(query_proj, angles)
        .astype(jnp.bfloat16)
        .reshape(row_count, KV_HEADS, repeat, HEAD_DIM)
    )
    key_proj = matmul(normed, full_key).reshape(row_count, KV_HEADS, HEAD_DIM)
    keys_own = rotary(key_proj, angles).astype(jnp.bfloat16).reshape(row_count, KV_WIDTH)
    values_own = matmul(normed, full_value).astype(jnp.bfloat16)
    all_keys, all_values = (
        lax.all_gather(keys_own, "ctx", axis=0, tiled=True),
        lax.all_gather(values_own, "ctx", axis=0, tiled=True),
    )
    packed_keys = jnp.take(
        all_keys.reshape(block_total, BLOCK, KV_WIDTH), stored_of_packed, axis=0
    ).reshape(group_total, KV_HEADS, HEAD_DIM)
    packed_values = jnp.take(
        all_values.reshape(block_total, BLOCK, KV_WIDTH), stored_of_packed, axis=0
    ).reshape(group_total, KV_HEADS, HEAD_DIM)

    def block_scores(block_index):
        start = block_index * BLOCK
        key_piece = lax.dynamic_slice_in_dim(packed_keys, start, BLOCK, 0)
        value_piece = lax.dynamic_slice_in_dim(packed_values, start, BLOCK, 0)
        key_logical = start + jnp.arange(BLOCK, dtype=jnp.int32)
        key_document = lax.dynamic_slice_in_dim(packed_document, start, BLOCK, 0)
        scores = (
            jnp.einsum("tgrd,ngd->grtn", queries, key_piece, preferred_element_type=jnp.float32)
            * score_scale
        )
        allowed = (own_document[:, None] == key_document[None, :]) & (
            key_logical[None, :] <= own_logical[:, None]
        )
        return (scores, allowed, key_piece, value_piece)

    def pass_total(block_index, state_pair):
        top_score, running = state_pair
        scores, allowed, _, _ = block_scores(block_index)
        scores = jnp.where(allowed, scores, -1e30)
        new_top = jnp.maximum(top_score, jnp.max(scores, axis=-1))
        expo = jnp.where(allowed, jnp.exp(scores - new_top[..., None]), 0.0)
        running = running * jnp.exp(top_score - new_top) + jnp.sum(expo, axis=-1)
        return (new_top, running)

    start_top = jnp.full((KV_HEADS, repeat, row_count), -1e30, jnp.float32)
    start_total = jnp.zeros((KV_HEADS, repeat, row_count), jnp.float32)
    top_score, running = lax.fori_loop(low_block, high_block, pass_total, (start_top, start_total))
    log_total = top_score + jnp.log(running)

    def pass_mix(block_index, accumulated):
        scores, allowed, _, value_piece = block_scores(block_index)
        probs = jnp.where(allowed, jnp.exp(scores - log_total[..., None]), 0.0).astype(jnp.bfloat16)
        return accumulated + jnp.einsum(
            "grtn,ngd->tgrd", probs, value_piece, preferred_element_type=jnp.float32
        )

    start_mix = jnp.zeros((row_count, KV_HEADS, repeat, HEAD_DIM), jnp.float32)
    mixed = lax.fori_loop(low_block, high_block, pass_mix, start_mix)
    attended = mixed.reshape(row_count, Q_WIDTH).astype(jnp.bfloat16)
    hidden = tokens + matmul(attended, full_output)
    inv_two = rms_scale(hidden)
    base_two = hidden * inv_two
    normed_two = (base_two * gains[1]).astype(jnp.bfloat16)
    gate = matmul(normed_two, full_gate)
    upward = matmul(normed_two, full_up)
    sigma = jax.nn.sigmoid(gate)
    inner = (gate * sigma * upward).astype(jnp.bfloat16)
    block_out = hidden + matmul(inner, full_down)
    back_query, back_key, back_value, back_output, back_gate, back_up, back_down = (
        full_query,
        full_key,
        full_value,
        full_output,
        full_gate,
        full_up,
        full_down,
    )
    grad_out = cotangent[0].astype(jnp.float32)
    grad_low = cotangent[0]
    grad_down = outer_sum(inner, grad_low)
    grad_inner = back_dot(grad_low, back_down)
    grad_gate_act = (grad_inner * upward * sigma * (1.0 + gate * (1.0 - sigma))).astype(
        jnp.bfloat16
    )
    grad_up_act = (grad_inner * gate * sigma).astype(jnp.bfloat16)
    grad_gate = outer_sum(normed_two, grad_gate_act)
    grad_up = outer_sum(normed_two, grad_up_act)
    grad_normed_two = back_dot(grad_gate_act, back_gate) + back_dot(grad_up_act, back_up)
    grad_hidden_norm, gain_two = norm_back(grad_normed_two, base_two, inv_two, gains[1])
    grad_hidden = grad_out + grad_hidden_norm
    hidden_low = grad_hidden.astype(jnp.bfloat16)
    grad_output = outer_sum(attended, hidden_low)
    grad_attended = back_dot(hidden_low, back_output).astype(jnp.bfloat16)
    grad_attended_heads = grad_attended.reshape(row_count, KV_HEADS, repeat, HEAD_DIM)
    delta = jnp.sum(grad_attended_heads.astype(jnp.float32) * mixed, axis=-1).transpose(1, 2, 0)

    def back_block(block_index, carry):
        grad_queries, grad_key_full, grad_value_full = carry
        scores, allowed, key_piece, value_piece = block_scores(block_index)
        probs = jnp.where(allowed, jnp.exp(scores - log_total[..., None]), 0.0)
        grad_probs = jnp.einsum(
            "tgrd,ngd->grtn", grad_attended_heads, value_piece, preferred_element_type=jnp.float32
        )
        grad_scores = (probs * (grad_probs - delta[..., None])).astype(jnp.bfloat16)
        grad_queries = (
            grad_queries
            + jnp.einsum(
                "grtn,ngd->tgrd", grad_scores, key_piece, preferred_element_type=jnp.float32
            )
            * score_scale
        )
        grad_key_piece = (
            jnp.einsum("grtn,tgrd->ngd", grad_scores, queries, preferred_element_type=jnp.float32)
            * score_scale
        )
        grad_value_piece = jnp.einsum(
            "grtn,tgrd->ngd",
            probs.astype(jnp.bfloat16),
            grad_attended_heads,
            preferred_element_type=jnp.float32,
        )
        start = block_index * BLOCK
        grad_key_full = lax.dynamic_update_slice_in_dim(
            grad_key_full, grad_key_piece.reshape(BLOCK, KV_WIDTH), start, 0
        )
        grad_value_full = lax.dynamic_update_slice_in_dim(
            grad_value_full, grad_value_piece.reshape(BLOCK, KV_WIDTH), start, 0
        )
        return (grad_queries, grad_key_full, grad_value_full)

    zero_rows = jnp.zeros((group_total, KV_WIDTH), jnp.float32)
    grad_queries, grad_key_full, grad_value_full = lax.fori_loop(
        low_block,
        high_block,
        back_block,
        (jnp.zeros((row_count, KV_HEADS, repeat, HEAD_DIM), jnp.float32), zero_rows, zero_rows),
    )
    grad_key_stored = jnp.take(
        grad_key_full.reshape(block_total, BLOCK, KV_WIDTH), arrangement, axis=0
    ).reshape(group_total, KV_WIDTH)
    grad_value_stored = jnp.take(
        grad_value_full.reshape(block_total, BLOCK, KV_WIDTH), arrangement, axis=0
    ).reshape(group_total, KV_WIDTH)
    grad_keys_own, grad_values_own = (
        lax.psum_scatter(
            grad_key_stored.astype(jnp.bfloat16), "ctx", scatter_dimension=0, tiled=True
        ).astype(jnp.float32),
        lax.psum_scatter(
            grad_value_stored.astype(jnp.bfloat16), "ctx", scatter_dimension=0, tiled=True
        ).astype(jnp.float32),
    )
    grad_query_proj = (
        rotary(grad_queries.reshape(row_count, HEADS, HEAD_DIM), -angles)
        .reshape(row_count, Q_WIDTH)
        .astype(jnp.bfloat16)
    )
    grad_key_proj = (
        rotary(grad_keys_own.reshape(row_count, KV_HEADS, HEAD_DIM), -angles)
        .reshape(row_count, KV_WIDTH)
        .astype(jnp.bfloat16)
    )
    grad_value_proj = grad_values_own.astype(jnp.bfloat16)
    grad_query = outer_sum(normed, grad_query_proj)
    grad_key = outer_sum(normed, grad_key_proj)
    grad_value = outer_sum(normed, grad_value_proj)
    grad_normed = (
        back_dot(grad_query_proj, back_query)
        + back_dot(grad_key_proj, back_key)
        + back_dot(grad_value_proj, back_value)
    )
    grad_input_norm, gain_one = norm_back(grad_normed, base_one, inv_one, gains[0])
    grad_input = grad_hidden + grad_input_norm
    dp_count = lax.axis_size("dp")
    ctx_count = lax.axis_size("ctx")
    grads_all = (grad_query, grad_key, grad_value, grad_output, grad_gate, grad_up, grad_down)
    split_all = tuple((grad.reshape(dp_count * ctx_count, -1) for grad in grads_all))
    owned = (
        lax.psum_scatter(split_all[0], ("dp", "ctx"), scatter_dimension=0, tiled=True),
        lax.psum_scatter(split_all[1], ("dp", "ctx"), scatter_dimension=0, tiled=True),
        lax.psum_scatter(split_all[2], ("dp", "ctx"), scatter_dimension=0, tiled=True),
        lax.psum_scatter(split_all[3], ("dp", "ctx"), scatter_dimension=0, tiled=True),
        lax.psum_scatter(split_all[4], ("dp", "ctx"), scatter_dimension=0, tiled=True),
        lax.psum_scatter(split_all[5], ("dp", "ctx"), scatter_dimension=0, tiled=True),
        lax.psum_scatter(split_all[6], ("dp", "ctx"), scatter_dimension=0, tiled=True),
    )
    grad_gains = lax.psum(jnp.stack([gain_one, gain_two]), ("dp", "ctx"))
    return (
        block_out[None],
        grad_input[None],
        owned[0].reshape(-1),
        owned[1].reshape(-1),
        owned[2].reshape(-1),
        owned[3].reshape(-1),
        owned[4].reshape(-1),
        owned[5].reshape(-1),
        owned[6].reshape(-1),
        grad_gains,
    )


def solution(mesh):
    return jax.shard_map(
        local,
        mesh=mesh,
        in_specs=(
            P("dp", "ctx", None),
            P("dp", "ctx", None),
            P(("dp", "ctx")),
            P(("dp", "ctx")),
            P(("dp", "ctx")),
            P(("dp", "ctx")),
            P(("dp", "ctx")),
            P(("dp", "ctx")),
            P(("dp", "ctx")),
            P(),
            P("dp", None),
            P("dp", None),
        ),
        out_specs=(
            P("dp", "ctx", None),
            P("dp", "ctx", None),
            P(("dp", "ctx")),
            P(("dp", "ctx")),
            P(("dp", "ctx")),
            P(("dp", "ctx")),
            P(("dp", "ctx")),
            P(("dp", "ctx")),
            P(("dp", "ctx")),
            P(),
        ),
        check_vma=False,
    )
```

profile of v0, /device:TPU:0, one launch (start us, length us, event | category | flops | bytes accessed | tf_op | source)
XLA Modules:
  0.0 1417.5 jit_solution(953967270961220893)
XLA Ops:
  10.2 77.3 %all-gather.1 = bf16[32,1,9600]{2,1,0:T(2,128)(2,1)S(1)} all-gather(bf16[1,1,9600]{2,1,0:T(2,128)(2,1)S(1)} %reshape.498), channel_id=1, replica_groups=mesh['dp'=4,'ctx'=8] {'dp','ctx'}, dimensions={0}, use_global_device_ids=true | all-gather | bytes 633600 | tf_op jit(solution)/shard_map/all_gather | solution.py:93
  94.4 73.9 %all-gather = bf16[32,1,9600]{2,1,0:T(2,128)(2,1)S(1)} all-gather(bf16[1,1,9600]{2,1,0:T(2,128)(2,1)S(1)} %reshape.496), channel_id=1, replica_groups=mesh['dp'=4,'ctx'=8] {'dp','ctx'}, dimensions={0}, use_global_device_ids=true | all-gather | bytes 633600 | tf_op jit(solution)/shard_map/all_gather | solution.py:94
  188.6 26.2 %all-gather.12.cloned.1.call-done = bf16[2048,320]{0,1:T(8,128)(2,1)} async-done(((bf16[256,320]{0,1:T(8,128)(2,1)}), bf16[2048,320]{0,1:T(8,128)(2,1)}) %all-gather.12.cloned.1.call-update) | async-done | bytes 1310736 | tf_op jit(solution)/shard_map/all_gather | solution.py:138
  227.2 50.5 %all-gather.22.cloned.1.call-done = bf16[32,1,28800]{2,1,0:T(2,128)(2,1)} async-done(((bf16[1,1,28800]{2,1,0:T(2,128)(2,1)}), bf16[32,1,28800]{2,1,0:T(2,128)(2,1)}) %all-gather.22.cloned.1.call-update) | async-done | bytes 1843216 | tf_op jit(solution)/shard_map/all_gather | solution.py:92
  277.7 40.8 %reduce.2 = bf16[32,28800]{1,0:T(8,128)(2,1)} reduce(bf16[32,1,28800]{2,1,0:T(2,128)(2,1)} %all-gather.22.cloned.1.call-done, bf16[]{:T(256)} %constant.154), dimensions={1}, to_apply=%all-gather.2.reduce_sub_computation | reduce | bytes 3686402 | tf_op jit(solution)/shard_map/all_gather | solution.py:92
  326.8 32.5 %while.36 = (s32[]{:T(128)}, f32[5,3,256]{2,1,0:T(4,128)S(1)}, f32[5,3,256]{2,1,0:T(4,128)S(1)}, s32[]{:T(128)}, s32[256]{0:T(256)S(1)}, /*index=5*/s32[2048]{0:...) while((s32[]{:T(128)}, f32[5,3,256]{2,1,0:T(4,128)S(1)}, ...), condition=%wide.region_11.13_spmd, body=%wide.region_8.12_spmd.sunk | while | flops 66952836 | bytes 4808383 | solution.py:173
  359.4 28.7 %while.37 = (s32[]{:T(128)}, f32[256,5,3,64]{0,3,2,1:T(8,128)S(1)}, s32[]{:T(128)}, bf16[2048,5,64]{0,2,1:T(8,128)(2,1)}, s32[256]{0:T(256)S(1)}, /*index=5*/s32...) while((s32[]{:T(128)}, f32[256,5,3,64]{0,3,2,1:T(8,128)S(1)}, ...), condition=%wide.region_13.15_spmd, body=%wide.region_12.14_spmd.sunk | while | flops 128139400 | bytes 2708163 | solution.py:184
  388.2 40.9 %reduce.3 = bf16[32,28800]{1,0:T(8,128)(2,1)} reduce(bf16[32,1,28800]{2,1,0:T(2,128)(2,1)} %all-gather.24.cloned.1.call-done, bf16[]{:T(256)} %constant.154), dimensions={1}, to_apply=%all-gather.3.reduce_sub_computation | reduce | bytes 3686402 | tf_op jit(solution)/shard_map/all_gather | solution.py:95
  435.9 10.1 reshape.434
  446.0 26.6 %all-gather.18.cloned.1.call-done = bf16[2457600]{0:T(1024)(128)(2,1)} async-done(((bf16[76800]{0:T(1024)(128)(2,1)}), bf16[2457600]{0:T(1024)(128)(2,1)}) %all-gather.18.cloned.1.call-update) | async-done | bytes 4915216 | tf_op jit(solution)/shard_map/all_gather | solution.py:97
  472.6 10.0 reshape.435
  491.3 47.3 %all-gather.20.cloned.1.call-done = bf16[2457600]{0:T(1024)(128)(2,1)} async-done(((bf16[76800]{0:T(1024)(128)(2,1)}), bf16[2457600]{0:T(1024)(128)(2,1)}) %all-gather.20.cloned.1.call-update) | async-done | bytes 4915216 | tf_op jit(solution)/shard_map/all_gather | solution.py:98
  538.7 9.5 reshape.436
  548.2 8.7 multiply_convert_fusion
  572.5 88.8 %while.38 = (s32[]{:T(128)}, f32[256,5,3,64]{0,3,2,1:T(8,128)S(1)}, bf16[2048,320]{0,1:T(8,128)(2,1)}, bf16[2048,320]{0,1:T(8,128)(2,1)}, s32[]{:T(128)}, /*inde...) while((s32[]{:T(128)}, f32[256,5,3,64]{0,3,2,1:T(8,128)S(1)}, ...), condition=%wide.region_18.20_spmd, body=%wide.region_17.19_spmd.sunk | while | flops 318685312 | bytes 13623027 | solution.py:258
  696.4 6.5 fusion.96
  702.9 10.3 reshape.451
  713.2 6.5 fusion.97
  719.8 10.5 reshape.453
  735.9 10.8 reshape.455
  750.0 64.0 %reduce-scatter.5.cloned.1.call-done = bf16[256,320]{0,1:T(8,128)(2,1)} async-done(((bf16[2048,320]{0,1:T(8,128)(2,1)}), bf16[256,320]{0,1:T(8,128)(2,1)}) %reduce-scatter.5.cloned.1.call-update) | async-done | bytes 163856 | tf_op jit(solution)/shard_map/reduce_scatter | solution.py:274
  820.7 5.7 fusion.45
  828.2 41.9 %psum.7 = f32[2,960]{1,0:T(2,128)} all-reduce(f32[2,960]{1,0:T(2,128)S(1)} %pad_maximum_fusion.4), channel_id=1, replica_groups=mesh['dp'=4,'ctx'=8] {'dp','ctx'}, use_global_device_ids=true, to_apply=%region_31.34 | all-reduce | flops 1920 | bytes 15360 | tf_op jit(solution)/shard_map/psum | solution.py:312
  871.3 528.1 %all-reduce.10.cloned.1.call-done = (f32[32,28800]{1,0:T(8,128)}, f32[32,9600]{1,0:T(8,128)}, f32[32,9600]{1,0:T(8,128)}, f32[32,28800]{1,0:T(8,128)}, f32[32,76...) async-done(((f32[32,28800]{1,0:T(8,128)}, f32[32,9600]{1,0:T(8,128)}, f32[32,9600]{1,0:T(8,128)}, f32[32,28800]{1,0:T(8,128)}, f32[32,76800]{1,0:T(8,128)}, ...) | async-done | bytes 39321616
  (503 shorter events, 288.3 us)
Async XLA Ops:
  7.2 178.0 %all-gather.14.cloned.1.call-start = ((), (), s32[]{:S(2)}) async-start(), calls=%async_computation.3 | async-start | bytes 1474560 | tf_op jit(solution)/shard_map/all_gather | solution.py:137
  94.4 120.4 %all-gather.12.cloned.1.call-start = ((), (), s32[]{:S(2)}) async-start(), calls=%async_computation.2 | async-start | bytes 1474560 | tf_op jit(solution)/shard_map/all_gather | solution.py:138
  172.0 11.8 copy-start.32
  172.8 12.3 copy-start.13
  174.2 103.6 %all-gather.22.cloned.1.call-start = ((), (), s32[]{:S(2)}) async-start(), calls=%async_computation.9 | async-start | bytes 3801600 | tf_op jit(solution)/shard_map/all_gather | solution.py:92
  175.0 213.3 %all-gather.24.cloned.1.call-start = ((), (), s32[]{:S(2)}) async-start(), calls=%async_computation.10 | async-start | bytes 3801600 | tf_op jit(solution)/shard_map/all_gather | solution.py:95
  175.7 260.2 %all-gather.16.cloned.1.call-start = ((), (), s32[]{:S(2)}) async-start(), calls=%async_computation.4 | async-start | bytes 5068800 | tf_op jit(solution)/shard_map/all_gather | solution.py:96
  176.3 296.3 %all-gather.18.cloned.1.call-start = ((), (), s32[]{:S(2)}) async-start(), calls=%async_computation.5 | async-start | bytes 5068800 | tf_op jit(solution)/shard_map/all_gather | solution.py:97
  176.9 361.8 %all-gather.20.cloned.1.call-start = ((), (), s32[]{:S(2)}) async-start(), calls=%async_computation.6 | async-start | bytes 5068800 | tf_op jit(solution)/shard_map/all_gather | solution.py:98
  177.7 569.0 %reduce-scatter.3.cloned.1.call-start = ((), (), s32[]{:S(2)}) async-start(), calls=%async_computation.7 | async-start | bytes 1474560 | tf_op jit(solution)/shard_map/reduce_scatter | solution.py:271
  388.1 41.1 %copy-start.4 = (f32[256,5,3,64]{0,3,2,1:T(8,128)}, f32[256,5,3,64]{0,3,2,1:T(8,128)S(1)}, u32[]{:S(2)}) copy-start(f32[256,5,3,64]{0,3,2,1:T(8,128)S(1)} %get-tuple-element.191) | copy-start | bytes 2949124
  388.1 41.1 %copy-start.28 = (f32[5,3,256]{2,1,0:T(4,128)}, f32[5,3,256]{2,1,0:T(4,128)S(1)}, u32[]{:S(2)}) copy-start(f32[5,3,256]{2,1,0:T(4,128)S(1)} %get-tuple-element.749) | copy-start | bytes 46084
  388.2 45.0 %copy-start.18 = (bf16[256,5,3,64]{0,3,2,1:T(8,128)(2,1)}, bf16[256,5,3,64]{0,3,2,1:T(8,128)(2,1)S(1)}, u32[]{:S(2)}) copy-start(bf16[256,5,3,64]{0,3,2,1:T(8,128)(2,1)S(1)} %convert_element_type.149) | copy-start | bytes 1474564
  435.7 126.0 %copy-start.11 = (f32[256,960]{0,1:T(8,128)}, f32[256,960]{0,1:T(8,128)S(1)}, u32[]{:S(2)}) copy-start(f32[256,960]{0,1:T(8,128)S(1)} %get-tuple-element.326) | copy-start | bytes 2949124
  482.6 5.7 copy-start
  491.3 56.9 %copy-start.15 = (bf16[1,256,960]{1,2,0:T(8,128)(2,1)S(1)}, bf16[1,256,960]{1,2,0:T(8,128)(2,1)}, u32[]{:S(2)}) copy-start(bf16[1,256,960]{1,2,0:T(8,128)(2,1)} %param.23) | copy-start | bytes 1474564
  556.9 4.8 copy-start.23
  556.9 4.8 copy-start.22
  676.8 137.2 %reduce-scatter.5.cloned.1.call-start = ((), (), s32[]{:S(2)}) async-start(), calls=%async_computation.8 | async-start | bytes 1474560 | tf_op jit(solution)/shard_map/reduce_scatter | solution.py:274
  679.9 719.5 %all-reduce.10.cloned.1.call-start = ((), (), s32[]{:S(2)}) async-start(), calls=%async_computation.11 | async-start | bytes 78643200
  683.3 5.4 copy-start.3
  683.3 5.4 copy-start.19
  719.8 10.5 copy-start.20
  820.7 5.7 copy-start.9
  (19 other events, 41.9 us)
Sparse Core Ops, SparseCore 0:
  94.5 44.5 all-gather.13
  174.3 40.4 all-gather.11
  218.3 59.3 all-gather.21
  281.1 59.6 all-gather.23
  343.5 63.1 all-gather.15
  409.4 63.1 all-gather.17
  475.5 63.1 all-gather.19
  677.0 69.7 reduce-scatter.2
  750.1 63.8 reduce-scatter.4
  820.3 579.0 all-reduce.9
where the time goes:
time: 1430 us; the launch traced here: 1420 us
  waiting for transfers between devices  745 us (52%)
  blocking collectives  193 us (13%)
  matrix products  189 us (13%)
  local copies, waits for them, and re-layouts  148 us (10%)
  other arithmetic  119 us (8%)
  between operations  20.2 us (1%)
    unnamed x11, waiting for transfers between devices  530 us
    all_gather x1, blocking collectives, local(): lax.all_gather(w_key, ('dp', 'ctx'), axis=0, tiled=True)  77.3 us
    all_gather x1, blocking collectives, local(): lax.all_gather(w_value, ('dp', 'ctx'), axis=0, tiled=True)  73.9 us
    reduce_scatter x1, waiting for transfers between devices, local(): lax.psum_scatter(grad_value_stored.astype(jnp.bfloat16), 'ctx', scatter_d...  64 us
    all_gather x1, waiting for transfers between devices, local(): lax.all_gather(w_query, ('dp', 'ctx'), axis=0, tiled=True)  50.5 us
    all_gather x1, waiting for transfers between devices, local(): lax.all_gather(w_down, ('dp', 'ctx'), axis=0, tiled=True)  47.3 us
    reshape x7, local copies, waits for them, and re-layouts, local(): grad.reshape(dp_count * ctx_count, -1)  45.8 us
    dot_general x30, matrix products, block_scores(): jnp.einsum('tgrd,ngd->grtn', queries, key_piece, preferred_element_type=j...  42.5 us
  transfers between devices with their start and end apart: 10, of which 6 were waited for; matrix products, arithmetic and copies ran while one was open for 21% of the time, Pallas kernels for 0%

commit v1 on v0

--- a/solution.py
+++ b/solution.py
@@ -88,18 +88,23 @@
     repeat = HEADS // KV_HEADS
     score_scale = HEAD_DIM ** (-0.5)
     shapes = ((D, Q_WIDTH), (D, KV_WIDTH), (D, KV_WIDTH), (Q_WIDTH, D), (D, FF), (D, FF), (FF, D))
-    gathered = (
-        lax.all_gather(w_query, ("dp", "ctx"), axis=0, tiled=True),
-        lax.all_gather(w_key, ("dp", "ctx"), axis=0, tiled=True),
-        lax.all_gather(w_value, ("dp", "ctx"), axis=0, tiled=True),
-        lax.all_gather(w_output, ("dp", "ctx"), axis=0, tiled=True),
-        lax.all_gather(w_gate, ("dp", "ctx"), axis=0, tiled=True),
-        lax.all_gather(w_up, ("dp", "ctx"), axis=0, tiled=True),
-        lax.all_gather(w_down, ("dp", "ctx"), axis=0, tiled=True),
-    )
-    full_query, full_key, full_value, full_output, full_gate, full_up, full_down = tuple(
-        (flat.reshape(shape_pair) for flat, shape_pair in zip(gathered, shapes))
-    )
+    axes = ("dp", "ctx")
+    by_rows = w_query.shape[0] % D == 0
+    if by_rows:
+        rows = w_query.shape[0] // D
+        local_one = jnp.concatenate(
+            [w.reshape(rows, -1) for w in (w_query, w_key, w_value, w_output)], axis=1
+        )
+        whole_one = lax.all_gather(local_one.reshape(-1), axes, axis=0, tiled=True).reshape(D, -1)
+        full_query = whole_one[:, :Q_WIDTH]
+        full_key = whole_one[:, Q_WIDTH : Q_WIDTH + KV_WIDTH]
+        full_value = whole_one[:, Q_WIDTH + KV_WIDTH : Q_WIDTH + 2 * KV_WIDTH]
+        full_output = whole_one[:, Q_WIDTH + 2 * KV_WIDTH :]
+    else:
+        full_query, full_key, full_value, full_output = tuple(
+            lax.all_gather(w, axes, axis=0, tiled=True).reshape(pair)
+            for w, pair in zip((w_query, w_key, w_value, w_output), shapes[:4])
+        )
     lengths = seq_lengths[0]
     arrangement = block_order[0]
     logical_all, document_all, position_all = token_tables(lengths, arrangement)
@@ -133,16 +138,26 @@
     key_proj = matmul(normed, full_key).reshape(row_count, KV_HEADS, HEAD_DIM)
     keys_own = rotary(key_proj, angles).astype(jnp.bfloat16).reshape(row_count, KV_WIDTH)
     values_own = matmul(normed, full_value).astype(jnp.bfloat16)
-    all_keys, all_values = (
-        lax.all_gather(keys_own, "ctx", axis=0, tiled=True),
-        lax.all_gather(values_own, "ctx", axis=0, tiled=True),
-    )
-    packed_keys = jnp.take(
-        all_keys.reshape(block_total, BLOCK, KV_WIDTH), stored_of_packed, axis=0
-    ).reshape(group_total, KV_HEADS, HEAD_DIM)
-    packed_values = jnp.take(
-        all_values.reshape(block_total, BLOCK, KV_WIDTH), stored_of_packed, axis=0
-    ).reshape(group_total, KV_HEADS, HEAD_DIM)
+    all_pairs = lax.all_gather(
+        jnp.concatenate([keys_own, values_own], axis=1), "ctx", axis=0, tiled=True
+    )
+    if by_rows:
+        local_two = jnp.concatenate([w.reshape(rows, -1) for w in (w_gate, w_up, w_down)], axis=1)
+        local_two, all_pairs = lax.optimization_barrier((local_two.reshape(-1), all_pairs))
+        whole_two = lax.all_gather(local_two, axes, axis=0, tiled=True).reshape(D, -1)
+        full_gate = whole_two[:, :FF]
+        full_up = whole_two[:, FF : 2 * FF]
+        full_down = whole_two[:, 2 * FF :].reshape(FF, D)
+    else:
+        full_gate, full_up, full_down = tuple(
+            lax.all_gather(w, axes, axis=0, tiled=True).reshape(pair)
+            for w, pair in zip((w_gate, w_up, w_down), shapes[4:])
+        )
+    packed_pairs = jnp.take(
+        all_pairs.reshape(block_total, BLOCK, 2 * KV_WIDTH), stored_of_packed, axis=0
+    ).reshape(group_total, 2 * KV_WIDTH)
+    packed_keys = packed_pairs[:, :KV_WIDTH].reshape(group_total, KV_HEADS, HEAD_DIM)
+    packed_values = packed_pairs[:, KV_WIDTH:].reshape(group_total, KV_HEADS, HEAD_DIM)
 
     def block_scores(block_index):
         start = block_index * BLOCK
@@ -217,6 +232,13 @@
     hidden_low = grad_hidden.astype(jnp.bfloat16)
     grad_output = outer_sum(attended, hidden_low)
     grad_attended = back_dot(hidden_low, back_output).astype(jnp.bfloat16)
+    def flat_low(parts):
+        return jnp.concatenate([part.astype(jnp.bfloat16).reshape(-1) for part in parts])
+
+    low_two, low_down, grad_attended = lax.optimization_barrier(
+        (flat_low((grad_gate, grad_up)), flat_low((grad_down,)), grad_attended)
+    )
+    sum_down = lax.psum(low_down, axes)
     grad_attended_heads = grad_attended.reshape(row_count, KV_HEADS, repeat, HEAD_DIM)
     delta = jnp.sum(grad_attended_heads.astype(jnp.float32) * mixed, axis=-1).transpose(1, 2, 0)
 
@@ -261,20 +283,16 @@
         back_block,
         (jnp.zeros((row_count, KV_HEADS, repeat, HEAD_DIM), jnp.float32), zero_rows, zero_rows),
     )
-    grad_key_stored = jnp.take(
-        grad_key_full.reshape(block_total, BLOCK, KV_WIDTH), arrangement, axis=0
-    ).reshape(group_total, KV_WIDTH)
-    grad_value_stored = jnp.take(
-        grad_value_full.reshape(block_total, BLOCK, KV_WIDTH), arrangement, axis=0
-    ).reshape(group_total, KV_WIDTH)
-    grad_keys_own, grad_values_own = (
-        lax.psum_scatter(
-            grad_key_stored.astype(jnp.bfloat16), "ctx", scatter_dimension=0, tiled=True
-        ).astype(jnp.float32),
-        lax.psum_scatter(
-            grad_value_stored.astype(jnp.bfloat16), "ctx", scatter_dimension=0, tiled=True
-        ).astype(jnp.float32),
-    )
+    grad_pairs = jnp.concatenate([grad_key_full, grad_value_full], axis=1).astype(jnp.bfloat16)
+    grad_pairs = jnp.take(
+        grad_pairs.reshape(block_total, BLOCK, 2 * KV_WIDTH), arrangement, axis=0
+    ).reshape(group_total, 2 * KV_WIDTH)
+    grad_pairs, sum_down = lax.optimization_barrier((grad_pairs, sum_down))
+    own_pairs = lax.psum_scatter(grad_pairs, "ctx", scatter_dimension=0, tiled=True)
+    own_pairs, low_two = lax.optimization_barrier((own_pairs, low_two))
+    sum_two = lax.psum(low_two, axes)
+    grad_keys_own = own_pairs[:, :KV_WIDTH].astype(jnp.float32)
+    grad_values_own = own_pairs[:, KV_WIDTH:].astype(jnp.float32)
     grad_query_proj = (
         rotary(grad_queries.reshape(row_count, HEADS, HEAD_DIM), -angles)
         .reshape(row_count, Q_WIDTH)
@@ -296,30 +314,37 @@
     )
     grad_input_norm, gain_one = norm_back(grad_normed, base_one, inv_one, gains[0])
     grad_input = grad_hidden + grad_input_norm
-    dp_count = lax.axis_size("dp")
-    ctx_count = lax.axis_size("ctx")
-    grads_all = (grad_query, grad_key, grad_value, grad_output, grad_gate, grad_up, grad_down)
-    split_all = tuple((grad.reshape(dp_count * ctx_count, -1) for grad in grads_all))
-    owned = (
-        lax.psum_scatter(split_all[0], ("dp", "ctx"), scatter_dimension=0, tiled=True),
-        lax.psum_scatter(split_all[1], ("dp", "ctx"), scatter_dimension=0, tiled=True),
-        lax.psum_scatter(split_all[2], ("dp", "ctx"), scatter_dimension=0, tiled=True),
-        lax.psum_scatter(split_all[3], ("dp", "ctx"), scatter_dimension=0, tiled=True),
-        lax.psum_scatter(split_all[4], ("dp", "ctx"), scatter_dimension=0, tiled=True),
-        lax.psum_scatter(split_all[5], ("dp", "ctx"), scatter_dimension=0, tiled=True),
-        lax.psum_scatter(split_all[6], ("dp", "ctx"), scatter_dimension=0, tiled=True),
-    )
-    grad_gains = lax.psum(jnp.stack([gain_one, gain_two]), ("dp", "ctx"))
+    rank = lax.axis_index("dp") * lax.axis_size("ctx") + lax.axis_index("ctx")
+
+    def own_parts(summed, sizes):
+        base, taken = 0, []
+        for size in sizes:
+            taken.append(
+                lax.dynamic_slice_in_dim(summed, base + rank * size, size).astype(jnp.float32)
+            )
+            base += size * device_count
+        return tuple(taken)
+
+    device_count = lax.axis_size("dp") * lax.axis_size("ctx")
+    own_gate, own_up = own_parts(sum_two, (w_gate.shape[0], w_up.shape[0]))
+    (own_down,) = own_parts(sum_down, (w_down.shape[0],))
+    low_one = flat_low((grad_query, grad_key, grad_value, grad_output, gain_one, gain_two))
+    low_one, own_gate = lax.optimization_barrier((low_one, own_gate))
+    sum_one = lax.psum(low_one, axes)
+    own_query, own_key, own_value, own_output = own_parts(
+        sum_one, (w_query.shape[0], w_key.shape[0], w_value.shape[0], w_output.shape[0])
+    )
+    grad_gains = sum_one[-2 * D :].astype(jnp.float32).reshape(2, D)
     return (
         block_out[None],
         grad_input[None],
-        owned[0].reshape(-1),
-        owned[1].reshape(-1),
-        owned[2].reshape(-1),
-        owned[3].reshape(-1),
-        owned[4].reshape(-1),
-        owned[5].reshape(-1),
-        owned[6].reshape(-1),
+        own_query,
+        own_key,
+        own_value,
+        own_output,
+        own_gate,
+        own_up,
+        own_down,
         grad_gains,
     )
 

time: 1430 us -> 993 us (0.69)
  waiting for transfers between devices: 745 us -> 498 us
  blocking collectives: 193 us -> 0 us
  local copies, waits for them, and re-layouts: 148 us -> 235 us
  other arithmetic: 119 us -> 52 us
  matrix products: 189 us -> 165 us
    unnamed x11 -> x7, waiting for transfers between devices: 530 us -> 0.11 us
    psum x0 -> x3, waiting for transfers between devices: none -> 285 us  [the longest x1 140 us: local(): sum_one = lax.psum(low_one, axes)]
    all_gather x2 -> x0, blocking collectives: 151 us -> none  [the longest x1 77.3 us: local(): lax.all_gather(w_key, ('dp', 'ctx'), axis=0, tiled=True)]
    all_gather x4 -> x0, other arithmetic: 89.1 us -> none  [the longest x1 40.9 us: local(): lax.all_gather(w_output, ('dp', 'ctx'), axis=0, tiled=True)]
    concatenate x0 -> x2, local copies, waits for them, and re-layouts: none -> 65.9 us  [the longest x1 65.8 us: flat_low(): jnp.concatenate([part.astype(jnp.bfloat16).reshape(-1) for part in parts])]
    psum x1 -> x0, blocking collectives: 41.9 us -> none  [local(): grad_gains = lax.psum(jnp.stack([gain_one, gain_two]), ('dp', 'ctx'))]
    concatenate x0 -> x4, other arithmetic: none -> 16.3 us  [the longest x1 11.2 us: flat_low(): jnp.concatenate([part.astype(jnp.bfloat16).reshape(-1) for part in parts])]
    all_gather x7 -> x3, waiting for transfers between devices: 151 us -> 143 us  [the longest x1 62.4 us: local(): lax.all_gather(local_one.reshape(-1), axes, axis=0, tiled=True)]
  transfers between devices with their start and end apart: 10 -> 7, of which waited for: 6 -> 7; matrix products, arithmetic and copies ran while one was open for 21% -> 29% of each run, Pallas kernels for 0% -> 0%
where the time goes in v1:
time: 993 us; the launch traced here: 974 us
  waiting for transfers between devices  498 us (50%)
  local copies, waits for them, and re-layouts  235 us (24%)
  matrix products  165 us (17%)
  other arithmetic  52 us (5%)
  between operations  20.4 us (2%)
    psum x1, waiting for transfers between devices, local(): sum_one = lax.psum(low_one, axes)  140 us
    psum x1, waiting for transfers between devices, local(): sum_two = lax.psum(low_two, axes)  109 us
    reduce_scatter x1, waiting for transfers between devices, local(): lax.psum_scatter(grad_pairs, 'ctx', scatter_dimension=0, tiled=True)  70.1 us
    concatenate x1, local copies, waits for them, and re-layouts, flat_low(): jnp.concatenate([part.astype(jnp.bfloat16).reshape(-1) for part in parts])  65.8 us
    all_gather x1, waiting for transfers between devices, local(): lax.all_gather(local_one.reshape(-1), axes, axis=0, tiled=True)  62.4 us
    all_gather x1, waiting for transfers between devices, local(): lax.all_gather(jnp.concatenate([keys_own, values_own], axis=1), 'ctx', ax...  53.7 us
    reshape x7, local copies, waits for them, and re-layouts, flat_low(): part.astype(jnp.bfloat16).reshape(-1)  49.5 us
    psum x1, waiting for transfers between devices, local(): sum_down = lax.psum(low_down, axes)  35.1 us
  transfers between devices with their start and end apart: 7, of which 7 were waited for; matrix products, arithmetic and copies ran while one was open for 29% of the time, Pallas kernels for 0%

profile of v1, /device:TPU:0, one launch (start us, length us, event | category | flops | bytes accessed | tf_op | source)
XLA Modules:
  0.0 974.2 jit_solution(11244668966120237720)
XLA Ops:
  16.7 62.4 %all-gather.4.cloned.1.call-done = bf16[2457600]{0:T(1024)(128)(2,1)} async-done(((bf16[76800]{0:T(1024)(128)(2,1)}), bf16[2457600]{0:T(1024)(128)(2,1)}) %all-gather.4.cloned.1.call-update) | async-done | bytes 4915216 | tf_op jit(solution)/shard_map/all_gather | solution.py:98
  79.0 10.0 %reshape.412 = bf16[960,2560]{1,0:T(8,128)(2,1)} reshape(bf16[2457600]{0:T(1024)(128)(2,1)} %all-gather.4.cloned.1.call-done) | data formatting | bytes 9830400 | tf_op jit(solution)/shard_map/reshape | solution.py:98
  96.1 53.7 %all-gather.6.cloned.1.call-done = bf16[2048,640]{0,1:T(8,128)(2,1)} async-done(((bf16[256,640]{0,1:T(8,128)(2,1)}), bf16[2048,640]{0,1:T(8,128)(2,1)}) %all-gather.6.cloned.1.call-update) | async-done | bytes 2621456 | tf_op jit(solution)/shard_map/all_gather | solution.py:141
  176.8 19.2 %while.36 = (s32[]{:T(128)}, f32[5,3,256]{2,1,0:T(4,128)S(1)}, f32[5,3,256]{2,1,0:T(4,128)S(1)}, s32[]{:T(128)}, s32[256]{0:T(256)S(1)}, /*index=5*/s32[2048]{0:...) while((s32[]{:T(128)}, f32[5,3,256]{2,1,0:T(4,128)S(1)}, ...), condition=%wide.region_11.13_spmd, body=%wide.region_8.12_spmd.sunk | while | flops 66952836 | bytes 4808383 | solution.py:188
  197.2 28.5 %while.37 = (s32[]{:T(128)}, f32[256,5,3,64]{0,3,2,1:T(8,128)S(1)}, s32[]{:T(128)}, bf16[2048,5,64]{0,2,1:T(8,128)(2,1)}, s32[256]{0:T(256)S(1)}, /*index=5*/s32...) while((s32[]{:T(128)}, f32[256,5,3,64]{0,3,2,1:T(8,128)S(1)}, ...), condition=%wide.region_13.15_spmd, body=%wide.region_12.14_spmd.sunk | while | flops 128139400 | bytes 2708163 | solution.py:199
  230.3 27.1 %all-gather.8.cloned.1.call-done = bf16[7372800]{0:T(1024)(128)(2,1)} async-done(((bf16[230400]{0:T(1024)(128)(2,1)}), bf16[7372800]{0:T(1024)(128)(2,1)}) %all-gather.8.cloned.1.call-update) | async-done | bytes 14745616 | tf_op jit(solution)/shard_map/all_gather | solution.py:147
  257.4 25.6 %reshape.417 = bf16[960,7680]{1,0:T(8,128)(2,1)} reshape(bf16[7372800]{0:T(1024)(128)(2,1)} %all-gather.8.cloned.1.call-done) | data formatting | bytes 29491200 | tf_op jit(solution)/shard_map/reshape | solution.py:147
  283.0 4.9 slice.116
  287.9 11.2 %reshape.418 = bf16[2560,960]{1,0:T(8,128)(2,1)} reshape(bf16[960,2560]{1,0:T(8,128)(2,1)} %slice.116) | data formatting | bytes 9830400 | tf_op jit(solution)/shard_map/reshape | solution.py:150
  304.8 7.0 multiply_convert_fusion.1
  323.6 18.5 %reshape.420 = bf16[2457600]{0:T(1024)(128)(2,1)} reshape(bf16[960,2560]{1,0:T(8,128)(2,1)} %convolution_convert_fusion.1) | data formatting | bytes 9830400 | tf_op jit(solution)/shard_map/reshape | solution.py:236
  342.1 10.3 %reshape.419 = bf16[2457600]{0:T(1024)(128)(2,1)} reshape(bf16[960,2560]{1,0:T(8,128)(2,1)} %convolution_convert_fusion.2) | data formatting | bytes 9830400 | tf_op jit(solution)/shard_map/reshape | solution.py:236
  352.4 4.9 convolution_convert_fusion
  357.3 7.8 copy.88
  365.2 10.5 %reshape.421 = bf16[2457600]{0:T(1024)(128)(2,1)} reshape(bf16[2560,960]{1,0:T(8,128)(2,1)} %copy.88) | data formatting | bytes 9830400 | tf_op jit(solution)/shard_map/reshape | solution.py:236
  379.8 11.2 %pad_maximum_fusion = bf16[4915200]{0:T(1024)(128)(2,1)} fusion(bf16[2457600]{0:T(1024)(128)(2,1)} %reshape.420, bf16[2457600]{0:T(1024)(128)(2,1)} %reshape.419), kind=kLoop, calls=%fused_computation.58 | loop fusion | flops 19660800 | bytes 19660800 | tf_op jit(solution)/shard_map/concatenate | solution.py:236
  393.8 89.0 %while.38 = (s32[]{:T(128)}, f32[256,5,3,64]{0,3,2,1:T(8,128)S(1)}, bf16[2048,320]{0,1:T(8,128)(2,1)}, bf16[2048,320]{0,1:T(8,128)(2,1)}, s32[]{:T(128)}, /*inde...) while((s32[]{:T(128)}, f32[256,5,3,64]{0,3,2,1:T(8,128)S(1)}, ...), condition=%wide.region_18.20_spmd, body=%wide.region_17.19_spmd.sunk | while | flops 318685312 | bytes 13623027 | solution.py:280
  500.1 35.1 %all-reduce.4.cloned.1.call-done = bf16[2457600]{0:T(1024)(128)(2,1)} async-done(((bf16[2457600]{0:T(1024)(128)(2,1)}), bf16[2457600]{0:T(1024)(128)(2,1)}) %all-reduce.4.cloned.1.call-update) | async-done | bytes 4915216 | tf_op jit(solution)/shard_map/psum | solution.py:241
  535.2 4.5 copy.91
  539.7 70.1 %reduce-scatter.2.cloned.1.call-done = bf16[256,640]{0,1:T(8,128)(2,1)} async-done(((bf16[2048,640]{0,1:T(8,128)(2,1)}), bf16[256,640]{0,1:T(8,128)(2,1)}) %reduce-scatter.2.cloned.1.call-update) | async-done | bytes 327696 | tf_op jit(solution)/shard_map/reduce_scatter | solution.py:291
  634.9 65.8 %concatenate.56 = bf16[2459520]{0:T(1024)(128)(2,1)} concatenate(bf16[921600]{0:T(1024)(128)(2,1)S(1)} %copy-done, bf16[307200]{0:T(1024)(128)(2,1)} %reshape.428, bf16[307200]{0:T(1024)(128)(2,1)} %reshape.429, bf16[921600]{0:T(1024)(128)(2,1)} %reshape.430, bf16[960]{0:T(1024)(128)(2,1)S(1)} %get-tuple-element.238, bf16[960]{0:T(1024)(128)(2,1)S(1)} %copy-done.18), dimensions={0} | concatenate | bytes 9838080 | tf_op jit(solution)/shard_map/concatenate | solution.py:236
  700.7 109.4 %all-reduce.6.cloned.1.call-done = bf16[4915200]{0:T(1024)(128)(2,1)} async-done(((bf16[4915200]{0:T(1024)(128)(2,1)}), bf16[4915200]{0:T(1024)(128)(2,1)}) %all-reduce.6.cloned.1.call-update) | async-done | bytes 9830416 | tf_op jit(solution)/shard_map/psum | solution.py:293
  813.1 6.0 fusion.63
  822.0 140.5 %all-reduce.8.cloned.1.call-done = bf16[2459520]{0:T(1024)(128)(2,1)} async-done(((bf16[2459520]{0:T(1024)(128)(2,1)}), bf16[2459520]{0:T(1024)(128)(2,1)}) %all-reduce.8.cloned.1.call-update) | async-done | bytes 4919056 | tf_op jit(solution)/shard_map/psum | solution.py:333
  (483 shorter events, 255.1 us)
Async XLA Ops:
  7.2 71.9 %all-gather.4.cloned.1.call-start = ((), (), s32[]{:S(2)}) async-start(), calls=%async_computation.1 | async-start | bytes 5068800 | tf_op jit(solution)/shard_map/all_gather | solution.py:98
  11.8 138.0 %all-gather.6.cloned.1.call-start = ((), (), s32[]{:S(2)}) async-start(), calls=%async_computation.2 | async-start | bytes 2949120 | tf_op jit(solution)/shard_map/all_gather | solution.py:141
  90.9 3.4 copy-start.15
  93.1 62.7 %copy-start.20 = (s32[1,16]{1,0:T(1,128)S(1)}, s32[1,16]{1,0:T(1,128)}, u32[]{:S(2)}) copy-start(s32[1,16]{1,0:T(1,128)} %param.31) | copy-start | bytes 196
  94.0 163.4 %all-gather.8.cloned.1.call-start = ((), (), s32[]{:S(2)}) async-start(), calls=%async_computation.3 | async-start | bytes 15206400 | tf_op jit(solution)/shard_map/all_gather | solution.py:147
  149.8 385.3 %all-reduce.4.cloned.1.call-start = ((), (), s32[]{:S(2)}) async-start(), calls=%async_computation.4 | async-start | bytes 9830400 | tf_op jit(solution)/shard_map/psum | solution.py:241
  197.2 29.2 %copy-start.3 = (bf16[1,256,960]{1,2,0:T(8,128)(2,1)S(1)}, bf16[1,256,960]{1,2,0:T(8,128)(2,1)}, u32[]{:S(2)}) copy-start(bf16[1,256,960]{1,2,0:T(8,128)(2,1)} %param.20) | copy-start | bytes 1474564
  226.4 3.8 copy-start.9
  230.1 90.5 %copy-start.4 = (f32[256,960]{0,1:T(8,128)}, f32[256,960]{0,1:T(8,128)S(1)}, u32[]{:S(2)}) copy-start(f32[256,960]{0,1:T(8,128)S(1)} %get-tuple-element.344) | copy-start | bytes 2949124
  299.1 4.1 copy-start.1
  299.1 4.1 copy-start.7
  303.2 8.6 slice-start
  303.2 8.6 slice-start.1
  304.8 7.0 slice-start.2
  304.8 7.0 slice-start.3
  342.1 10.3 %copy-start.8 = (bf16[1,256,960]{1,2,0:T(8,128)(2,1)S(1)}, bf16[1,256,960]{1,2,0:T(8,128)(2,1)}, u32[]{:S(2)}) copy-start(bf16[1,256,960]{1,2,0:T(8,128)(2,1)} %param.21) | copy-start | bytes 1474564
  391.2 218.7 %reduce-scatter.2.cloned.1.call-start = ((), (), s32[]{:S(2)}) async-start(), calls=%async_computation.5 | async-start | bytes 2949120 | tf_op jit(solution)/shard_map/reduce_scatter | solution.py:291
  492.3 4.2 copy-start.19
  539.7 270.4 %all-reduce.6.cloned.1.call-start = ((), (), s32[]{:S(2)}) async-start(), calls=%async_computation.6 | async-start | bytes 19660800 | tf_op jit(solution)/shard_map/psum | solution.py:293
  609.9 352.6 %all-reduce.8.cloned.1.call-start = ((), (), s32[]{:S(2)}) async-start(), calls=%async_computation.7 | async-start | bytes 9838592 | tf_op jit(solution)/shard_map/psum | solution.py:333
  620.3 3.9 slice-start.4
  630.0 4.8 copy-start
  630.0 4.8 copy-start.18
  813.1 7.7 copy-start.11
  (9 other events, 14.5 us)
Sparse Core Ops, SparseCore 0:
  11.9 67.0 all-gather.3
  94.1 55.6 all-gather.5
  153.2 104.1 all-gather.7
  391.3 143.8 all-reduce.3
  539.8 70.0 reduce-scatter.1
  615.6 194.3 all-reduce.5
  816.7 145.6 all-reduce.7
